TPU v7x, 128 devices: a whole 4x4x4 slice. The times are simulated.
128 devices in a mesh: ctx: 16 (over x, y_lo, core), head: 8 (over y_hi, z).
Axes of the slice: x: 4, y: 4 (y_hi: 2, y_lo: 2; y = y_hi * 2 + y_lo), z: 4, core: 2. Of those that a mesh axis runs over, the one named last changes fastest.
Arguments:
- q_nope: bfloat16 [4096, 4096], P('ctx', 'head'), may hold values from -5 to 5
- q_rope: bfloat16 [4096, 2048], P('ctx', 'head'), may hold values from -320 to 320
- latent: bfloat16 [4096, 512], P('ctx'), may hold values from -5 to 5
- rope_keys: bfloat16 [4096, 64], P('ctx'), may hold values from -4.5 to 4.5
- out_grad: bfloat16 [4096, 4096], P('ctx', 'head'), may hold values from -96 to 96
- up_keys: bfloat16 [512, 4096], P(None, 'head'), may hold values from -0.25 to 0.25
- up_values: bfloat16 [512, 4096], P(None, 'head'), may hold values from -0.25 to 0.25
- group_order: int32 [32], replicated, may hold values from 0 to 31, each once
Outputs:
- grad_q_nope: bfloat16 [4096, 4096], P('ctx', 'head')
- grad_q_rope: bfloat16 [4096, 2048], P('ctx', 'head')
- grad_latent: float32 [4096, 512], P('ctx')
- grad_rope: float32 [4096, 64], P('ctx')
- grad_up_keys: float32 [512, 4096], P('ctx', 'head')
- grad_up_values: float32 [512, 4096], P('ctx', 'head')
Inputs may be any that keep to these rules, and one draw needn't show every extreme that they name: `group_order`: each group place appears once.
All inputs are finite; a program needn't handle non-finite values.
Results may differ from a plain program's by a relative error of at most 0.0087.
Values may be sent and summed in bfloat16 or wider, within the bound.
A program may use at most 128 MiB of HBM per device.

v0:
```python
import math
import jax
import jax.numpy as jnp
from jax import lax
from jax.sharding import PartitionSpec as P

ROPE = 64
HEAD_DIM = 128
H_DEV = 4
GROUP = 128
NEG_LARGE = -1e30


def positions(group_order, first_row, count):
    rows = first_row + jnp.arange(count, dtype=jnp.int32)
    group_ids = rows // GROUP
    table = jnp.arange(group_order.shape[0], dtype=jnp.int32)
    placed = jnp.sum(
        jnp.where(group_ids[:, None] == table[None, :], group_order[None, :], 0), axis=1
    )
    return placed * GROUP + rows % GROUP


def per_device(q_nope, q_rope, latent, rope_keys, out_grad, up_keys, up_values, group_order):
    width = q_nope.shape[0]
    scale = (HEAD_DIM + ROPE) ** (-0.5)
    seq_len = lax.axis_size("ctx") * width
    q_pos = positions(group_order, lax.axis_index("ctx") * width, width)
    query_nope = q_nope.reshape(width, H_DEV, HEAD_DIM)
    query_rope = q_rope.reshape(width, H_DEV, ROPE)
    grad_heads = out_grad.reshape(width, H_DEV, HEAD_DIM)
    pair_cols = 2 * H_DEV * HEAD_DIM
    latent_all, rope_all = (
        lax.all_gather(latent, "ctx", axis=0, tiled=True),
        lax.all_gather(rope_keys, "ctx", axis=0, tiled=True),
    )
    keys_all = jnp.dot(latent_all, up_keys, preferred_element_type=jnp.float32).astype(jnp.bfloat16)
    values_all = jnp.dot(latent_all, up_values, preferred_element_type=jnp.float32).astype(
        jnp.bfloat16
    )

    def fetch(start, count):
        key_rows = lax.dynamic_slice_in_dim(keys_all, start, count, 0).reshape(
            count, H_DEV, HEAD_DIM
        )
        value_rows = lax.dynamic_slice_in_dim(values_all, start, count, 0).reshape(
            count, H_DEV, HEAD_DIM
        )
        rope_rows = lax.dynamic_slice_in_dim(rope_all, start, count, 0)
        return (key_rows, value_rows, rope_rows)

    def block_scores(key_rows, rope_rows, k_pos):
        raw = jnp.einsum("thd,khd->htk", query_nope, key_rows, preferred_element_type=jnp.float32)
        raw = raw + jnp.einsum(
            "thr,kr->htk", query_rope, rope_rows, preferred_element_type=jnp.float32
        )
        visible = (k_pos[None, :] <= q_pos[:, None])[None]
        return (jnp.where(visible, raw * scale, NEG_LARGE), visible)

    block = math.gcd(seq_len, 512)
    block_count = seq_len // block

    def stats_visit(carry, index):
        start = index * block
        k_pos = positions(group_order, start, block)
        row_top, row_total, weighted = carry
        key_rows, value_rows, rope_rows = fetch(start, block)
        score, visible = block_scores(key_rows, rope_rows, k_pos)
        dattn = jnp.einsum(
            "thd,khd->htk", grad_heads, value_rows, preferred_element_type=jnp.float32
        )
        new_top = jnp.maximum(row_top, jnp.max(score, axis=2))
        factor = jnp.exp(row_top - new_top)
        expd = jnp.where(visible, jnp.exp(score - new_top[..., None]), 0.0)
        new_total = row_total * factor + jnp.sum(expd, axis=2)
        new_weighted = weighted * factor + jnp.sum(expd * dattn, axis=2)
        carry = (new_top, new_total, new_weighted)
        return (carry, None)

    start_top = jnp.full((H_DEV, width), NEG_LARGE, jnp.float32)
    zeros_rows = jnp.zeros((H_DEV, width), jnp.float32)
    row_top, row_total, weighted = lax.scan(
        stats_visit, (start_top, zeros_rows, zeros_rows), jnp.arange(block_count, dtype=jnp.int32)
    )[0]
    delta = weighted / row_total

    def grad_visit(carry, index):
        start = index * block
        k_pos = positions(group_order, start, block)
        acc_nope, acc_rope = carry
        key_rows, value_rows, rope_rows = fetch(start, block)
        score, visible = block_scores(key_rows, rope_rows, k_pos)
        attn = jnp.where(visible, jnp.exp(score - row_top[..., None]) / row_total[..., None], 0.0)
        dattn = jnp.einsum(
            "thd,khd->htk", grad_heads, value_rows, preferred_element_type=jnp.float32
        )
        dscore = (attn * (dattn - delta[..., None])).astype(jnp.bfloat16)
        acc_nope = acc_nope + jnp.einsum(
            "htk,khd->thd", dscore, key_rows, preferred_element_type=jnp.float32
        )
        acc_rope = acc_rope + jnp.einsum(
            "htk,kr->thr", dscore, rope_rows, preferred_element_type=jnp.float32
        )
        dkey = (
            jnp.einsum("htk,thd->khd", dscore, query_nope, preferred_element_type=jnp.float32)
            * scale
        )
        dvalue = jnp.einsum(
            "htk,thd->khd",
            attn.astype(jnp.bfloat16),
            grad_heads,
            preferred_element_type=jnp.float32,
        )
        drope = (
            jnp.einsum("htk,thr->kr", dscore, query_rope, preferred_element_type=jnp.float32)
            * scale
        )
        pair_terms = jnp.stack([dkey, dvalue], axis=1).reshape(block, pair_cols)
        return ((acc_nope, acc_rope), (pair_terms, drope))

    start_nope = jnp.zeros((width, H_DEV, HEAD_DIM), jnp.float32)
    start_rope = jnp.zeros((width, H_DEV, ROPE), jnp.float32)
    (acc_nope, acc_rope), (pair_stack, rope_stack) = lax.scan(
        grad_visit, (start_nope, start_rope), jnp.arange(block_count, dtype=jnp.int32)
    )
    grad_q_nope = (acc_nope * scale).astype(jnp.bfloat16).reshape(width, H_DEV * HEAD_DIM)
    grad_q_rope = (acc_rope * scale).astype(jnp.bfloat16).reshape(width, H_DEV * ROPE)
    pair_sum, rope_part = (
        lax.psum_scatter(
            pair_stack.reshape(seq_len, pair_cols), "ctx", scatter_dimension=0, tiled=True
        ),
        lax.psum_scatter(rope_stack.reshape(seq_len, ROPE), "ctx", scatter_dimension=0, tiled=True),
    )
    pair_sum = pair_sum.reshape(width, 2, H_DEV * HEAD_DIM)
    dkeys = pair_sum[:, 0].astype(jnp.bfloat16)
    dvalues = pair_sum[:, 1].astype(jnp.bfloat16)
    contract_cols = (((1,), (1,)), ((), ()))
    latent_part = lax.dot_general(dkeys, up_keys, contract_cols, preferred_element_type=jnp.float32)
    latent_part = latent_part + lax.dot_general(
        dvalues, up_values, contract_cols, preferred_element_type=jnp.float32
    )
    grad_latent, grad_rope = lax.psum((latent_part, rope_part), "head")
    contract_rows = (((0,), (0,)), ((), ()))
    weight_keys = lax.dot_general(latent, dkeys, contract_rows, preferred_element_type=jnp.float32)
    weight_values = lax.dot_general(
        latent, dvalues, contract_rows, preferred_element_type=jnp.float32
    )
    grad_up_keys, grad_up_values = (
        lax.psum_scatter(weight_keys, "ctx", scatter_dimension=0, tiled=True),
        lax.psum_scatter(weight_values, "ctx", scatter_dimension=0, tiled=True),
    )
    return (grad_q_nope, grad_q_rope, grad_latent, grad_rope, grad_up_keys, grad_up_values)


def solution(mesh):
    in_specs = (
        P("ctx", "head"),
        P("ctx", "head"),
        P("ctx", None),
        P("ctx", None),
        P("ctx", "head"),
        P(None, "head"),
        P(None, "head"),
        P(),
    )
    out_specs = (
        P("ctx", "head"),
        P("ctx", "head"),
        P("ctx", None),
        P("ctx", None),
        P("ctx", "head"),
        P("ctx", "head"),
    )
    return jax.shard_map(
        per_device, mesh=mesh, in_specs=in_specs, out_specs=out_specs, check_vma=False
    )
```

profile of v0, /device:TPU:0, one launch (start us, length us, event | category | flops | bytes accessed | tf_op | source)
XLA Modules:
  0.0 750.5 jit_solution(6171262483542442688)
XLA Ops:
  11.8 22.9 %all_gather.7 = bf16[4096,64]{0,1:T(8,128)(2,1)} all-gather(bf16[256,64]{0,1:T(8,128)(2,1)S(1)} %copy-done.6), channel_id=1, replica_groups=mesh['ctx'=16,'head'=8] {'ctx'}, dimensions={0}, use_global_device_ids=true | all-gather | bytes 557056 | tf_op jit(solution)/shard_map/all_gather | solution.py:35
  34.7 15.2 %all-gather.2.cloned.1.call-done = bf16[4096,512]{1,0:T(8,128)(2,1)} async-done(((bf16[256,512]{1,0:T(8,128)(2,1)}), bf16[4096,512]{1,0:T(8,128)(2,1)}) %all-gather.2.cloned.1.call-update) | async-done | bytes 4194320 | tf_op jit(solution)/shard_map/all_gather | solution.py:34
  49.9 6.5 convolution_convert_fusion
  56.4 6.4 copy.104
  62.7 6.5 convolution_convert_fusion.1
  69.2 6.4 copy.106
  75.6 47.8 %while.36 = (s32[]{:T(128)}, f32[4,256]{1,0:T(4,128)S(1)}, f32[4,256]{1,0:T(4,128)S(1)}, f32[4,256]{1,0:T(4,128)S(1)}, s32[8]{0:T(128)S(1)}, /*index=5*/s32[32]{...) while((s32[]{:T(128)}, f32[4,256]{1,0:T(4,128)S(1)}, ...), condition=%wide.region_6.7_spmd.clone, body=%wide.region_1.6_spmd.clone.sunk | while | flops 341513728 | bytes 14964090 | solution.py:82
  123.5 158.1 %while.37 = (s32[]{:T(128)}, f32[256,4,128]{0,2,1:T(8,128)}, f32[256,4,64]{0,2,1:T(8,128)}, f32[8,512,1024]{2,1,0:T(8,128)}, f32[8,512,64]{1,0,2:T(8,128)}, /*in...) while((s32[]{:T(128)}, f32[256,4,128]{0,2,1:T(8,128)}, ...), condition=%wide.region_9.10_spmd.clone, body=%wide.region_7.9_spmd.clone.sunk | while | flops 879065600 | bytes 38036900 | solution.py:123
  137.0 3.8 dynamic_update_slice.20
  148.2 2.2 fusion.135
  156.9 3.8 dynamic_update_slice.20
  168.1 2.2 fusion.135
  176.8 3.8 dynamic_update_slice.20
  196.7 3.8 dynamic_update_slice.20
  216.6 3.8 dynamic_update_slice.20
  236.6 3.8 dynamic_update_slice.20
  256.5 3.8 dynamic_update_slice.20
  267.7 2.2 fusion.135
  276.4 3.8 dynamic_update_slice.20
  284.5 174.1 %reduce-scatter.9.cloned.1.call-done = f32[256,1024]{1,0:T(8,128)} async-done(((f32[4096,1024]{1,0:T(8,128)}), f32[256,1024]{1,0:T(8,128)}) %reduce-scatter.9.cloned.1.call-update) | async-done | bytes 1048592 | tf_op jit(solution)/shard_map/reduce_scatter | solution.py:129
  462.5 65.2 %reduce-scatter.11.cloned.1.call-done = f32[256,64]{0,1:T(8,128)} async-done(((f32[4096,64]{0,1:T(8,128)}), f32[256,64]{0,1:T(8,128)}) %reduce-scatter.11.cloned.1.call-update) | async-done | bytes 65552 | tf_op jit(solution)/shard_map/reduce_scatter | solution.py:132
  535.0 80.0 %all-reduce.3.cloned.1.call-done = (f32[256,512]{1,0:T(8,128)}, f32[256,64]{0,1:T(8,128)}) async-done(((f32[256,512]{1,0:T(8,128)}, f32[256,64]{0,1:T(8,128)}), (f32[256,512]{1,0:T(8,128)}, f32[256,64]{0,1:T(8,128)})) %all-reduce.3.cloned.1.call-update) | async-done | bytes 589840 | tf_op jit(solution)/shard_map/psum | solution.py:142
  615.0 62.4 %reduce-scatter.15.cloned.1.call-done = f32[32,512]{1,0:T(8,128)} async-done(((f32[512,512]{1,0:T(8,128)}), f32[32,512]{1,0:T(8,128)}) %reduce-scatter.15.cloned.1.call-update) | async-done | bytes 65552
  677.4 62.9 %reduce-scatter.13.cloned.1.call-done = f32[32,512]{1,0:T(8,128)} async-done(((f32[512,512]{1,0:T(8,128)}), f32[32,512]{1,0:T(8,128)}) %reduce-scatter.13.cloned.1.call-update) | async-done | bytes 65552
  (305 shorter events, 179.5 us)
Async XLA Ops:
  7.2 55.6 %copy-start = (bf16[512,512]{1,0:T(8,128)(2,1)S(1)}, bf16[512,512]{1,0:T(8,128)(2,1)}, u32[]{:S(2)}) copy-start(bf16[512,512]{1,0:T(8,128)(2,1)} %param.17) | copy-start | bytes 1572868
  7.2 4.5 copy-start.5
  7.2 4.6 copy-start.6
  7.2 42.7 %copy-start.3 = (bf16[512,512]{1,0:T(8,128)(2,1)S(1)}, bf16[512,512]{1,0:T(8,128)(2,1)}, u32[]{:S(2)}) copy-start(bf16[512,512]{1,0:T(8,128)(2,1)} %param.18) | copy-start | bytes 1572868
  7.2 42.7 %all-gather.2.cloned.1.call-start = ((), (), s32[]{:S(2)}) async-start(), calls=%async_computation.4 | async-start | bytes 4456448 | tf_op jit(solution)/shard_map/all_gather | solution.py:34
  7.9 450.6 %reduce-scatter.9.cloned.1.call-start = ((), (), s32[]{:S(2)}) async-start(), calls=%async_computation.5 | async-start | bytes 17825792 | tf_op jit(solution)/shard_map/reduce_scatter | solution.py:129
  281.6 1.2 copy-start.2
  281.6 246.1 %reduce-scatter.11.cloned.1.call-start = ((), (), s32[]{:S(2)}) async-start(), calls=%async_computation.6 | async-start | bytes 1114112 | tf_op jit(solution)/shard_map/reduce_scatter | solution.py:132
  284.5 330.5 %all-reduce.3.cloned.1.call-start = ((), (), s32[]{:S(2)}) async-start(), calls=%async_computation.9 | async-start | bytes 1179648 | tf_op jit(solution)/shard_map/psum | solution.py:142
  459.9 1.5 copy-start.4
  461.0 66.8 %copy-start.1 = (bf16[256,512]{1,0:T(8,128)(2,1)S(1)}, bf16[256,512]{1,0:T(8,128)(2,1)}, u32[]{:S(2)}) copy-start(bf16[256,512]{1,0:T(8,128)(2,1)} %param.14) | copy-start | bytes 786436
  527.8 149.6 %reduce-scatter.15.cloned.1.call-start = ((), (), s32[]{:S(2)}) async-start(), calls=%async_computation.8 | async-start | bytes 1114112
  529.6 210.8 %reduce-scatter.13.cloned.1.call-start = ((), (), s32[]{:S(2)}) async-start(), calls=%async_computation.7 | async-start | bytes 1114112
Sparse Core Ops, SparseCore 0:
  9.8 40.0 all-gather.1
  281.8 176.7 reduce-scatter.8
  461.0 66.7 reduce-scatter.10
  530.3 84.6 all-reduce.2
  617.9 59.4 reduce-scatter.14
  680.2 60.1 reduce-scatter.12
where the time goes:
time: 754 us; the launch traced here: 751 us
  waiting for transfers between devices  461 us (61%)
  local copies, waits for them, and re-layouts  116 us (15%)
  matrix products  102 us (14%)
  other arithmetic  23.3 us (3%)
  blocking collectives  22.9 us (3%)
  between operations  14.4 us (2%)
  loops' own time  11.6 us (2%)
    reduce_scatter x1, waiting for transfers between devices, per_device(): lax.psum_scatter(pair_stack.reshape(seq_len, pair_cols), 'ctx', scatter_d...  174 us
    unnamed x8, waiting for transfers between devices  126 us
    psum x1, waiting for transfers between devices, per_device(): grad_latent, grad_rope = lax.psum((latent_part, rope_part), 'head')  80 us
    reduce_scatter x1, waiting for transfers between devices, per_device(): lax.psum_scatter(rope_stack.reshape(seq_len, ROPE), 'ctx', scatter_dimens...  65.2 us
    dynamic_update_slice x32, local copies, waits for them, and re-layouts, per_device(): lax.scan(grad_visit, (start_nope, start_rope), jnp.arange(block_count, dt...  58.2 us
    unnamed x27, local copies, waits for them, and re-layouts  25.7 us
    dot_general x16, matrix products, block_scores(): jnp.einsum('thr,kr->htk', query_rope, rope_rows, preferred_element_type=j...  25.4 us
    all_gather x1, blocking collectives, per_device(): lax.all_gather(rope_keys, 'ctx', axis=0, tiled=True)  22.9 us
  transfers between devices with their start and end apart: 6, of which 6 were waited for; matrix products, arithmetic and copies ran while one was open for 2% of the time, Pallas kernels for 0%

commit v1 on v0

--- a/solution.py
+++ b/solution.py
@@ -9,6 +9,9 @@
 H_DEV = 4
 GROUP = 128
 NEG_LARGE = -1e30
+skins_apply = lambda here_x: jnp.concatenate(
+    lax.all_to_all(jnp.stack([here_x for _ in range(lax.axis_size("ctx"))], 0), "ctx", 0, 0), 0
+)
 
 
 def positions(group_order, first_row, count):
@@ -31,7 +34,7 @@
     grad_heads = out_grad.reshape(width, H_DEV, HEAD_DIM)
     pair_cols = 2 * H_DEV * HEAD_DIM
     latent_all, rope_all = (
-        lax.all_gather(latent, "ctx", axis=0, tiled=True),
+        skins_apply(latent),
         lax.all_gather(rope_keys, "ctx", axis=0, tiled=True),
     )
     keys_all = jnp.dot(latent_all, up_keys, preferred_element_type=jnp.float32).astype(jnp.bfloat16)

time: 754 us -> 794 us (1.053)
  blocking collectives: 22.9 us -> 73.1 us
  waiting for transfers between devices: 461 us -> 444 us
    all_gather x1, blocking collectives: 22.9 us -> 73.1 us  [per_device(): lax.all_gather(rope_keys, 'ctx', axis=0, tiled=True)]
    all_gather x1 -> x0, waiting for transfers between devices: 15.2 us -> none  [per_device(): lax.all_gather(latent, 'ctx', axis=0, tiled=True)]
    unnamed x27 -> x33, local copies, waits for them, and re-layouts: 25.7 us -> 23.1 us
    unnamed x8 -> x7, waiting for transfers between devices: 126 us -> 125 us
  transfers between devices with their start and end apart: 6 -> 6, of which waited for: 6 -> 5; matrix products, arithmetic and copies ran while one was open for 2% -> 2% of each run, Pallas kernels for 0% -> 0%
where the time goes in v1:
time: 794 us; the launch traced here: 790 us
  waiting for transfers between devices  444 us (56%)
  local copies, waits for them, and re-layouts  116 us (15%)
  matrix products  102 us (13%)
  blocking collectives  73.1 us (9%)
  other arithmetic  23.2 us (3%)
  between operations  14.1 us (2%)
  loops' own time  11.6 us (1%)
    reduce_scatter x1, waiting for transfers between devices, per_device(): lax.psum_scatter(pair_stack.reshape(seq_len, pair_cols), 'ctx', scatter_d...  174 us
    unnamed x7, waiting for transfers between devices  125 us
    psum x1, waiting for transfers between devices, per_device(): grad_latent, grad_rope = lax.psum((latent_part, rope_part), 'head')  80.4 us
    all_gather x1, blocking collectives, per_device(): lax.all_gather(rope_keys, 'ctx', axis=0, tiled=True)  73.1 us
    reduce_scatter x1, waiting for transfers between devices, per_device(): lax.psum_scatter(rope_stack.reshape(seq_len, ROPE), 'ctx', scatter_dimens...  64.6 us
    dynamic_update_slice x32, local copies, waits for them, and re-layouts, per_device(): lax.scan(grad_visit, (start_nope, start_rope), jnp.arange(block_count, dt...  58.2 us
    dot_general x16, matrix products, block_scores(): jnp.einsum('thr,kr->htk', query_rope, rope_rows, preferred_element_type=j...  25.4 us
    unnamed x33, local copies, waits for them, and re-layouts  23.1 us
  transfers between devices with their start and end apart: 6, of which 5 were waited for; matrix products, arithmetic and copies ran while one was open for 2% of the time, Pallas kernels for 0%

profile of v1, /device:TPU:0, one launch (start us, length us, event | category | flops | bytes accessed | tf_op | source)
XLA Modules:
  0.0 790.4 jit_solution(812736082041090265)
XLA Ops:
  7.2 3.4 stack.17
  10.5 5.7 all-to-all-start
  17.3 73.1 %all_gather.3 = bf16[4096,64]{0,1:T(8,128)(2,1)} all-gather(bf16[256,64]{0,1:T(8,128)(2,1)S(1)} %copy-done.9), channel_id=1, replica_groups=mesh['ctx'=16,'head'=8] {'ctx'}, dimensions={0}, use_global_device_ids=true | all-gather | bytes 557056 | tf_op jit(solution)/shard_map/all_gather | solution.py:38
  90.4 6.5 convolution_convert_fusion
  96.9 6.4 copy.104
  103.3 6.5 convolution_convert_fusion.1
  109.8 6.4 copy.106
  116.2 47.9 %while.36 = (s32[]{:T(128)}, f32[4,256]{1,0:T(4,128)S(1)}, f32[4,256]{1,0:T(4,128)S(1)}, f32[4,256]{1,0:T(4,128)S(1)}, s32[8]{0:T(128)S(1)}, /*index=5*/s32[32]{...) while((s32[]{:T(128)}, f32[4,256]{1,0:T(4,128)S(1)}, ...), condition=%wide.region_6.7_spmd.clone, body=%wide.region_1.6_spmd.clone.sunk | while | flops 341513728 | bytes 14964090 | solution.py:85
  164.1 158.0 %while.37 = (s32[]{:T(128)}, f32[256,4,128]{0,2,1:T(8,128)}, f32[256,4,64]{0,2,1:T(8,128)}, f32[8,512,1024]{2,1,0:T(8,128)}, f32[8,512,64]{1,0,2:T(8,128)}, /*in...) while((s32[]{:T(128)}, f32[256,4,128]{0,2,1:T(8,128)}, ...), condition=%wide.region_9.10_spmd.clone, body=%wide.region_7.9_spmd.clone.sunk | while | flops 879065600 | bytes 38036900 | solution.py:126
  177.6 3.8 dynamic_update_slice.20
  188.8 2.2 fusion.135
  197.5 3.8 dynamic_update_slice.20
  217.4 3.8 dynamic_update_slice.20
  237.3 3.8 dynamic_update_slice.20
  248.5 2.2 fusion.135
  257.2 3.8 dynamic_update_slice.20
  277.1 3.8 dynamic_update_slice.20
  297.0 3.8 dynamic_update_slice.20
  316.9 3.8 dynamic_update_slice.20
  325.2 173.9 %reduce-scatter.9.cloned.1.call-done = f32[256,1024]{1,0:T(8,128)} async-done(((f32[4096,1024]{1,0:T(8,128)}), f32[256,1024]{1,0:T(8,128)}) %reduce-scatter.9.cloned.1.call-update) | async-done | bytes 1048592 | tf_op jit(solution)/shard_map/reduce_scatter | solution.py:132
  503.1 64.6 %reduce-scatter.11.cloned.1.call-done = f32[256,64]{0,1:T(8,128)} async-done(((f32[4096,64]{0,1:T(8,128)}), f32[256,64]{0,1:T(8,128)}) %reduce-scatter.11.cloned.1.call-update) | async-done | bytes 65552 | tf_op jit(solution)/shard_map/reduce_scatter | solution.py:135
  574.8 80.4 %all-reduce.3.cloned.1.call-done = (f32[256,512]{1,0:T(8,128)}, f32[256,64]{0,1:T(8,128)}) async-done(((f32[256,512]{1,0:T(8,128)}, f32[256,64]{0,1:T(8,128)}), (f32[256,512]{1,0:T(8,128)}, f32[256,64]{0,1:T(8,128)})) %all-reduce.3.cloned.1.call-update) | async-done | bytes 589840 | tf_op jit(solution)/shard_map/psum | solution.py:145
  655.2 62.4 %reduce-scatter.15.cloned.1.call-done = f32[32,512]{1,0:T(8,128)} async-done(((f32[512,512]{1,0:T(8,128)}), f32[32,512]{1,0:T(8,128)}) %reduce-scatter.15.cloned.1.call-update) | async-done | bytes 65552
  717.6 62.9 %reduce-scatter.13.cloned.1.call-done = f32[32,512]{1,0:T(8,128)} async-done(((f32[512,512]{1,0:T(8,128)}), f32[32,512]{1,0:T(8,128)}) %reduce-scatter.13.cloned.1.call-update) | async-done | bytes 65552
  (311 shorter events, 178.2 us)
Async XLA Ops:
  7.2 96.1 %copy-start = (bf16[512,512]{1,0:T(8,128)(2,1)S(1)}, bf16[512,512]{1,0:T(8,128)(2,1)}, u32[]{:S(2)}) copy-start(bf16[512,512]{1,0:T(8,128)(2,1)} %param.17) | copy-start | bytes 1572868
  10.5 5.9 copy-start.7
  10.5 6.0 copy-start.5
  10.5 6.3 copy-start.6
  10.5 79.9 %all-to-all-start = ((bf16[16,256,512]{2,1,0:T(8,128)(2,1)}), bf16[16,256,512]{2,1,0:T(8,128)(2,1)}, u32[]{:S(2)}, u32[]{:S(2)}) async-start(bf16[16,256,512]{2,1,0:T(8,128)(2,1)} %stack.17), calls=%async_computation | async-start | bytes 8388608 | tf_op jit(solution)/shard_map/all_to_all | solution.py:13
  16.2 0.9 copy-start.8
  16.2 1.0 copy-start.9
  16.3 74.2 %copy-start.3 = (bf16[512,512]{1,0:T(8,128)(2,1)S(1)}, bf16[512,512]{1,0:T(8,128)(2,1)}, u32[]{:S(2)}) copy-start(bf16[512,512]{1,0:T(8,128)(2,1)} %param.18) | copy-start | bytes 1572868
  16.3 482.8 %reduce-scatter.9.cloned.1.call-start = ((), (), s32[]{:S(2)}) async-start(), calls=%async_computation.5 | async-start | bytes 17825792 | tf_op jit(solution)/shard_map/reduce_scatter | solution.py:132
  322.1 1.2 copy-start.2
  322.1 245.5 %reduce-scatter.11.cloned.1.call-start = ((), (), s32[]{:S(2)}) async-start(), calls=%async_computation.6 | async-start | bytes 1114112 | tf_op jit(solution)/shard_map/reduce_scatter | solution.py:135
  325.0 330.2 %all-reduce.3.cloned.1.call-start = ((), (), s32[]{:S(2)}) async-start(), calls=%async_computation.9 | async-start | bytes 1179648 | tf_op jit(solution)/shard_map/psum | solution.py:145
  500.4 1.5 copy-start.4
  501.5 66.2 %copy-start.1 = (bf16[256,512]{1,0:T(8,128)(2,1)S(1)}, bf16[256,512]{1,0:T(8,128)(2,1)}, u32[]{:S(2)}) copy-start(bf16[256,512]{1,0:T(8,128)(2,1)} %param.14) | copy-start | bytes 786436
  567.7 149.9 %reduce-scatter.15.cloned.1.call-start = ((), (), s32[]{:S(2)}) async-start(), calls=%async_computation.8 | async-start | bytes 1114112
  569.4 211.1 %reduce-scatter.13.cloned.1.call-start = ((), (), s32[]{:S(2)}) async-start(), calls=%async_computation.7 | async-start | bytes 1114112
Sparse Core Ops, SparseCore 0:
  322.3 176.8 reduce-scatter.8
  501.5 66.0 reduce-scatter.10
  570.4 84.7 all-reduce.2
  658.1 59.4 reduce-scatter.14
  720.4 60.1 reduce-scatter.12
